TPU v7x, 256 devices: a whole 4x4x8 slice. The times are simulated.
256 devices in a mesh: tm: 8 (over y, core), mp: 4 (over z_lo), tok: 8 (over z_hi, x).
Axes of the slice: x: 4, y: 4, z: 8 (z_hi: 2, z_lo: 4; z = z_hi * 4 + z_lo), core: 2. Of those that a mesh axis runs over, the one named last changes fastest.
Arguments:
- features: bfloat16 [1024, 3584], P('tok'), may hold values from -6 to 6
- spike_mask: int32 [8, 1024, 3584], P('tm', 'tok'), may hold values 0 or 1
- gate_weight: bfloat16 [3584, 7168], P(('tm', 'tok'), 'mp'), may hold values from -0.09375 to 0.09375
- threshold: float32 [7168], P('mp'), may hold values from 0.5 to 2
Outputs:
- rates: float32 [1024, 7168], P('tok', 'mp')
- grad_threshold: float32 [7168], P('mp')
All inputs are finite; a program needn't handle non-finite values. No bound on the sum of `spike_mask` on one device may be relied on, other than what follows from the above.
Results may differ from a plain program's by a relative error of at most 0.00035.
Values may be sent and summed in bfloat16 or wider, within the bound.
No kernel may reach another device: no remote copies, remote signals or barrier semaphores. Data moves between devices by JAX's collectives and lax.ppermute only.
A program may use at most 64 MiB of HBM per device.

v0:
```python
import jax
import jax.numpy as jnp
from jax import lax
from jax.sharding import PartitionSpec as P

SHARP = 2.0


def passed_along(x, axis, by):
    peers = lax.axis_size(axis)
    pairs = [(i, i + by) for i in range(peers) if 0 <= i + by < peers]
    return lax.ppermute(x, axis, pairs)


def on_device(features, spike_mask, gate_weight, threshold):
    steps = lax.axis_size("tm")
    step_index = lax.axis_index("tm")
    tokens_all = features.shape[0] * lax.axis_size("tok")
    rows = features.shape[0]
    width = gate_weight.shape[1]
    driven = jnp.where(spike_mask[0] > 0, features, jnp.zeros_like(features))
    piece = lax.all_gather(gate_weight, ("tm", "tok"), axis=0, tiled=True)
    student = jnp.dot(driven, piece, preferred_element_type=jnp.float32)
    teacher = jnp.dot(features, piece, preferred_element_type=jnp.float32)
    current = 2.0 * student
    target = jax.nn.silu(teacher)
    blocks = 1
    size = rows // blocks
    turns = steps + blocks - 1

    def forward_turn(turn, carry):
        incoming, spikes = carry
        block = turn - step_index
        active = (block >= 0) & (block < blocks)
        rising = incoming + current
        fired = jax.nn.sigmoid(SHARP * (rising - threshold))
        leaving = rising - threshold * fired
        older = spikes
        spikes = jnp.where(active, fired, older)
        passed = passed_along(leaving, "tm", 1)
        return (passed, spikes)

    block_zero = jnp.zeros((size, width), jnp.float32)
    unused, spikes = lax.fori_loop(
        0, turns, forward_turn, (block_zero, jnp.zeros((rows, width), jnp.float32))
    )
    total = lax.psum(spikes, "tm")
    rates = threshold * total / steps
    error = (rates - target) / tokens_all

    def backward_turn(turn, carry):
        incoming, grad_sum = carry
        block = turn - (steps - 1 - step_index)
        active = (block >= 0) & (block < blocks)
        dspike = error * threshold / steps - threshold * incoming
        dwide = dspike * SHARP * spikes * (1.0 - spikes)
        term = jnp.sum(-dwide - spikes * incoming + error * spikes / steps, axis=0)
        grad_sum = grad_sum + jnp.where(active, term, jnp.zeros_like(term))
        passed = passed_along((incoming + dwide).astype(jnp.bfloat16), "tm", -1).astype(jnp.float32)
        return (passed, grad_sum)

    unused_cot, grad_local = lax.fori_loop(
        0, turns, backward_turn, (block_zero, jnp.zeros((width,), jnp.float32))
    )
    grad_threshold = lax.psum(grad_local, ("tm", "tok"))
    return (rates, grad_threshold)


def solution(mesh):
    return jax.shard_map(
        on_device,
        mesh=mesh,
        in_specs=(P("tok", None), P("tm", "tok", None), P(("tm", "tok"), "mp"), P("mp")),
        out_specs=(P("tok", "mp"), P("mp")),
        check_vma=False,
    )
```

profile of v0, /device:TPU:32, one launch (start us, length us, event | category | flops | bytes accessed | tf_op | source)
XLA Modules:
  0.0 676.2 jit_solution(10581541776726929995)
XLA Ops:
  8.0 140.1 %all-gather.2.cloned.1.call-done = bf16[3584,1792]{1,0:T(8,128)(2,1)} async-done(((bf16[56,1792]{1,0:T(8,128)(2,1)}), bf16[3584,1792]{1,0:T(8,128)(2,1)}) %all-gather.2.cloned.1.call-update) | async-done | bytes 12845072 | tf_op jit(solution)/shard_map/all_gather | solution.py:22
  148.0 7.4 %convolution_multiply_fusion = f32[128,1792]{1,0:T(8,128)S(1)} fusion(bf16[3584,1792]{1,0:T(8,128)(2,1)} %all-gather.2.cloned.1.call-done, bf16[128,3584]{1,0:T(8,128)(2,1)} %param.8, s32[1,128,3584]{2,1,0:T(8,128)} %param.9), kind=kOutput, calls=%fused_computation.8 | convolution fusion | flops 1645314048 | bytes 16515072 | tf_op jit(solution)/shard_map/dot_general | solution.py:23
  155.5 120.2 %while.34 = (s32[]{:T(128)}, f32[128,1792]{1,0:T(8,128)S(1)}, f32[128,1792]{1,0:T(8,128)S(1)}, f32[128,1792]{1,0:T(8,128)S(1)}, f32[1792]{0:T(1024)S(1)}, /*index=5*/s32[]{:T(128)}, s32[]{:T(128)}, s32[]{:T(128)}) while((s32[]{:T(128)}, f32[128,1792]{1,0:T(8,128)S(1)}, f32[128,1792]{1,0:T(8,128)S(1)}, f32[128,1792]{1,0:T(8,128)S(1)}, ...), condition=%wide.region_1.2_spmd.clone, body=%wide.region_0.1_spmd.clone.sunk | while | flops 2293767 | bytes 8264873 | solution.py:44
  155.5 1.5 select_select_fusion.2
  157.1 2.2 collective-permute-start
  159.3 2.2 collective-permute-done
  163.1 11.6 %collective-permute-start = (f32[128,1792]{1,0:T(8,128)}, f32[128,1792]{1,0:T(8,128)S(1)}, u32[]{:S(2)}, u32[]{:S(2)}) collective-permute-start(f32[128,1792]{1,0:T(8,128)} %get-tuple-element.455), channel_id=1, source_target_pairs={{0,32},{32,64},{64,96},{96,128},{128,160},{160,192},{192,224},{1,3... | collective-permute-start | bytes 2752520 | tf_op jit(solution)/shard_map/while/body/eval_jaxpr/ppermute | solution.py:12
  174.7 2.2 collective-permute-done
  176.9 1.5 select_select_fusion.2
  178.4 12.7 %collective-permute-start = (f32[128,1792]{1,0:T(8,128)}, f32[128,1792]{1,0:T(8,128)S(1)}, u32[]{:S(2)}, u32[]{:S(2)}) collective-permute-start(f32[128,1792]{1,0:T(8,128)} %get-tuple-element.455), channel_id=1, source_target_pairs={{0,32},{32,64},{64,96},{96,128},{128,160},{160,192},{192,224},{1,3... | collective-permute-start | bytes 2752520 | tf_op jit(solution)/shard_map/while/body/eval_jaxpr/ppermute | solution.py:12
  191.1 2.2 collective-permute-done
  194.9 12.7 %collective-permute-start = (f32[128,1792]{1,0:T(8,128)}, f32[128,1792]{1,0:T(8,128)S(1)}, u32[]{:S(2)}, u32[]{:S(2)}) collective-permute-start(f32[128,1792]{1,0:T(8,128)} %get-tuple-element.455), channel_id=1, source_target_pairs={{0,32},{32,64},{64,96},{96,128},{128,160},{160,192},{192,224},{1,3... | collective-permute-start | bytes 2752520 | tf_op jit(solution)/shard_map/while/body/eval_jaxpr/ppermute | solution.py:12
  207.6 2.2 collective-permute-done
  211.4 12.7 %collective-permute-start = (f32[128,1792]{1,0:T(8,128)}, f32[128,1792]{1,0:T(8,128)S(1)}, u32[]{:S(2)}, u32[]{:S(2)}) collective-permute-start(f32[128,1792]{1,0:T(8,128)} %get-tuple-element.455), channel_id=1, source_target_pairs={{0,32},{32,64},{64,96},{96,128},{128,160},{160,192},{192,224},{1,3... | collective-permute-start | bytes 2752520 | tf_op jit(solution)/shard_map/while/body/eval_jaxpr/ppermute | solution.py:12
  224.0 2.2 collective-permute-done
  227.8 12.7 %collective-permute-start = (f32[128,1792]{1,0:T(8,128)}, f32[128,1792]{1,0:T(8,128)S(1)}, u32[]{:S(2)}, u32[]{:S(2)}) collective-permute-start(f32[128,1792]{1,0:T(8,128)} %get-tuple-element.455), channel_id=1, source_target_pairs={{0,32},{32,64},{64,96},{96,128},{128,160},{160,192},{192,224},{1,3... | collective-permute-start | bytes 2752520 | tf_op jit(solution)/shard_map/while/body/eval_jaxpr/ppermute | solution.py:12
  240.5 2.2 collective-permute-done
  244.3 12.7 %collective-permute-start = (f32[128,1792]{1,0:T(8,128)}, f32[128,1792]{1,0:T(8,128)S(1)}, u32[]{:S(2)}, u32[]{:S(2)}) collective-permute-start(f32[128,1792]{1,0:T(8,128)} %get-tuple-element.455), channel_id=1, source_target_pairs={{0,32},{32,64},{64,96},{96,128},{128,160},{160,192},{192,224},{1,3... | collective-permute-start | bytes 2752520 | tf_op jit(solution)/shard_map/while/body/eval_jaxpr/ppermute | solution.py:12
  256.9 2.2 collective-permute-done
  260.7 12.7 %collective-permute-start = (f32[128,1792]{1,0:T(8,128)}, f32[128,1792]{1,0:T(8,128)S(1)}, u32[]{:S(2)}, u32[]{:S(2)}) collective-permute-start(f32[128,1792]{1,0:T(8,128)} %get-tuple-element.455), channel_id=1, source_target_pairs={{0,32},{32,64},{64,96},{96,128},{128,160},{160,192},{192,224},{1,3... | collective-permute-start | bytes 2752520 | tf_op jit(solution)/shard_map/while/body/eval_jaxpr/ppermute | solution.py:12
  273.4 2.2 collective-permute-done
  276.7 74.4 %all-reduce.2.cloned.1.call-done = f32[128,1792]{1,0:T(8,128)} async-done(((f32[128,1792]{1,0:T(8,128)}), f32[128,1792]{1,0:T(8,128)}) %all-reduce.2.cloned.1.call-update) | async-done | bytes 917520 | tf_op jit(solution)/shard_map/psum | solution.py:47
  351.1 8.4 %fusion.4 = (f32[128,1792]{1,0:T(8,128)S(1)}, f32[128,1792]{1,0:T(8,128)S(1)}, f32[128,1792]{1,0:T(8,128)}) fusion(f32[128,1792]{1,0:T(8,128)} %copy-done, f32[128,1792]{1,0:T(8,128)} %all-reduce.2.cloned.1.call-done, f32[1792]{0:T(1024)S(1)} %get-tuple-element.528, bf16[128,3584]{1,0:T(8,128)(2,1)} %param.8, ...), kind=kOutput, calls=%fused_computation.16 | convolution fusion | flops 1646231552 | bytes 18357248 | tf_op jit(solution)/shard_map/dot_general | solution.py:24
  359.4 99.1 %while.35 = (s32[]{:T(128)}, f32[128,1792]{1,0:T(8,128)}, f32[1792]{0:T(1024)S(1)}, f32[1792]{0:T(1024)S(1)}, f32[128,1792]{1,0:T(8,128)S(1)}, /*index=5*/f32[12...) while((s32[]{:T(128)}, f32[128,1792]{1,0:T(8,128)}, ...), condition=%wide.region_5.6_spmd.clone, body=%wide.region_3.5_spmd.clone.sunk | while | flops 4132359 | bytes 7376058 | solution.py:62
  361.3 2.5 collective-permute-done.1
  363.8 2.0 convert_element_type.22
  365.8 1.7 add_reduce_fusion.2
  368.8 5.9 collective-permute-done.1
  374.7 2.0 convert_element_type.22
  376.8 1.7 add_reduce_fusion.2
  379.8 8.6 %collective-permute-done.1 = bf16[128,1792]{1,0:T(8,128)(2,1)} collective-permute-done((bf16[128,1792]{1,0:T(8,128)(2,1)S(1)}, bf16[128,1792]{1,0:T(8,128)(2,1)}, u32[]{:S(2)}, u32[]{:S(2)}) %collective-permute-start.1) | collective-permute-done | bytes 458784 | tf_op jit(solution)/shard_map/while/body/eval_jaxpr/ppermute | solution.py:12
  388.4 2.0 convert_element_type.22
  390.4 1.7 add_reduce_fusion.2
  393.4 8.6 %collective-permute-done.1 = bf16[128,1792]{1,0:T(8,128)(2,1)} collective-permute-done((bf16[128,1792]{1,0:T(8,128)(2,1)S(1)}, bf16[128,1792]{1,0:T(8,128)(2,1)}, u32[]{:S(2)}, u32[]{:S(2)}) %collective-permute-start.1) | collective-permute-done | bytes 458784 | tf_op jit(solution)/shard_map/while/body/eval_jaxpr/ppermute | solution.py:12
  402.0 2.0 convert_element_type.22
  404.0 1.7 add_reduce_fusion.2
  407.0 8.6 %collective-permute-done.1 = bf16[128,1792]{1,0:T(8,128)(2,1)} collective-permute-done((bf16[128,1792]{1,0:T(8,128)(2,1)S(1)}, bf16[128,1792]{1,0:T(8,128)(2,1)}, u32[]{:S(2)}, u32[]{:S(2)}) %collective-permute-start.1) | collective-permute-done | bytes 458784 | tf_op jit(solution)/shard_map/while/body/eval_jaxpr/ppermute | solution.py:12
  415.6 2.0 convert_element_type.22
  417.6 1.7 add_reduce_fusion.2
  420.7 8.6 %collective-permute-done.1 = bf16[128,1792]{1,0:T(8,128)(2,1)} collective-permute-done((bf16[128,1792]{1,0:T(8,128)(2,1)S(1)}, bf16[128,1792]{1,0:T(8,128)(2,1)}, u32[]{:S(2)}, u32[]{:S(2)}) %collective-permute-start.1) | collective-permute-done | bytes 458784 | tf_op jit(solution)/shard_map/while/body/eval_jaxpr/ppermute | solution.py:12
  429.2 2.0 convert_element_type.22
  431.3 1.7 add_reduce_fusion.2
  434.3 8.6 %collective-permute-done.1 = bf16[128,1792]{1,0:T(8,128)(2,1)} collective-permute-done((bf16[128,1792]{1,0:T(8,128)(2,1)S(1)}, bf16[128,1792]{1,0:T(8,128)(2,1)}, u32[]{:S(2)}, u32[]{:S(2)}) %collective-permute-start.1) | collective-permute-done | bytes 458784 | tf_op jit(solution)/shard_map/while/body/eval_jaxpr/ppermute | solution.py:12
  442.9 2.0 convert_element_type.22
  444.9 1.7 add_reduce_fusion.2
  447.9 8.6 %collective-permute-done.1 = bf16[128,1792]{1,0:T(8,128)(2,1)} collective-permute-done((bf16[128,1792]{1,0:T(8,128)(2,1)S(1)}, bf16[128,1792]{1,0:T(8,128)(2,1)}, u32[]{:S(2)}, u32[]{:S(2)}) %collective-permute-start.1) | collective-permute-done | bytes 458784 | tf_op jit(solution)/shard_map/while/body/eval_jaxpr/ppermute | solution.py:12
  456.5 2.0 convert_element_type.22
  458.5 210.8 %psum.15 = f32[1792]{0:T(1024)} all-reduce(f32[1792]{0:T(1024)S(1)} %get-tuple-element.289), channel_id=1, replica_groups=mesh['tm'=8,'mp'=4,'tok'=8] {'tm','tok'}, use_global_device_ids=true, to_apply=%region_6.7 | all-reduce | flops 1792 | bytes 14336 | tf_op jit(solution)/shard_map/psum | solution.py:65
  (37 shorter events, 22.0 us)
Async XLA Ops:
  7.2 140.9 %all-gather.2.cloned.1.call-start = ((), (), s32[]{:S(2)}) async-start(), calls=%async_computation | async-start | bytes 13045760 | tf_op jit(solution)/shard_map/all_gather | solution.py:22
  7.9 343.2 %all-reduce.2.cloned.1.call-start = ((), (), s32[]{:S(2)}) async-start(), calls=%async_computation.1 | async-start | bytes 1835008 | tf_op jit(solution)/shard_map/psum | solution.py:47
  8.0 147.5 %copy-start.2 = (f32[1792]{0:T(1024)S(1)}, f32[1792]{0:T(1024)}, u32[]{:S(2)}) copy-start(f32[1792]{0:T(1024)} %param.11) | copy-start | bytes 21508
  157.1 4.5 collective-permute-start
  163.1 13.8 %collective-permute-start = (f32[128,1792]{1,0:T(8,128)}, f32[128,1792]{1,0:T(8,128)S(1)}, u32[]{:S(2)}, u32[]{:S(2)}) collective-permute-start(f32[128,1792]{1,0:T(8,128)} %get-tuple-element.455), channel_id=1, source_target_pairs={{0,32},{32,64},{64,96},{96,128},{128,160},{160,192},{192,224},{1,3... | collective-permute-start | bytes 2752520 | tf_op jit(solution)/shard_map/while/body/eval_jaxpr/ppermute | solution.py:12
  178.4 14.9 %collective-permute-start = (f32[128,1792]{1,0:T(8,128)}, f32[128,1792]{1,0:T(8,128)S(1)}, u32[]{:S(2)}, u32[]{:S(2)}) collective-permute-start(f32[128,1792]{1,0:T(8,128)} %get-tuple-element.455), channel_id=1, source_target_pairs={{0,32},{32,64},{64,96},{96,128},{128,160},{160,192},{192,224},{1,3... | collective-permute-start | bytes 2752520 | tf_op jit(solution)/shard_map/while/body/eval_jaxpr/ppermute | solution.py:12
  194.9 14.9 %collective-permute-start = (f32[128,1792]{1,0:T(8,128)}, f32[128,1792]{1,0:T(8,128)S(1)}, u32[]{:S(2)}, u32[]{:S(2)}) collective-permute-start(f32[128,1792]{1,0:T(8,128)} %get-tuple-element.455), channel_id=1, source_target_pairs={{0,32},{32,64},{64,96},{96,128},{128,160},{160,192},{192,224},{1,3... | collective-permute-start | bytes 2752520 | tf_op jit(solution)/shard_map/while/body/eval_jaxpr/ppermute | solution.py:12
  211.4 14.9 %collective-permute-start = (f32[128,1792]{1,0:T(8,128)}, f32[128,1792]{1,0:T(8,128)S(1)}, u32[]{:S(2)}, u32[]{:S(2)}) collective-permute-start(f32[128,1792]{1,0:T(8,128)} %get-tuple-element.455), channel_id=1, source_target_pairs={{0,32},{32,64},{64,96},{96,128},{128,160},{160,192},{192,224},{1,3... | collective-permute-start | bytes 2752520 | tf_op jit(solution)/shard_map/while/body/eval_jaxpr/ppermute | solution.py:12
  227.8 14.9 %collective-permute-start = (f32[128,1792]{1,0:T(8,128)}, f32[128,1792]{1,0:T(8,128)S(1)}, u32[]{:S(2)}, u32[]{:S(2)}) collective-permute-start(f32[128,1792]{1,0:T(8,128)} %get-tuple-element.455), channel_id=1, source_target_pairs={{0,32},{32,64},{64,96},{96,128},{128,160},{160,192},{192,224},{1,3... | collective-permute-start | bytes 2752520 | tf_op jit(solution)/shard_map/while/body/eval_jaxpr/ppermute | solution.py:12
  244.3 14.9 %collective-permute-start = (f32[128,1792]{1,0:T(8,128)}, f32[128,1792]{1,0:T(8,128)S(1)}, u32[]{:S(2)}, u32[]{:S(2)}) collective-permute-start(f32[128,1792]{1,0:T(8,128)} %get-tuple-element.455), channel_id=1, source_target_pairs={{0,32},{32,64},{64,96},{96,128},{128,160},{160,192},{192,224},{1,3... | collective-permute-start | bytes 2752520 | tf_op jit(solution)/shard_map/while/body/eval_jaxpr/ppermute | solution.py:12
  260.7 14.9 %collective-permute-start = (f32[128,1792]{1,0:T(8,128)}, f32[128,1792]{1,0:T(8,128)S(1)}, u32[]{:S(2)}, u32[]{:S(2)}) collective-permute-start(f32[128,1792]{1,0:T(8,128)} %get-tuple-element.455), channel_id=1, source_target_pairs={{0,32},{32,64},{64,96},{96,128},{128,160},{160,192},{192,224},{1,3... | collective-permute-start | bytes 2752520 | tf_op jit(solution)/shard_map/while/body/eval_jaxpr/ppermute | solution.py:12
  275.6 1.0 copy-start
  276.7 82.8 %copy-start.1 = (f32[128,1792]{1,0:T(8,128)S(1)}, f32[128,1792]{1,0:T(8,128)}, u32[]{:S(2)}) copy-start(f32[128,1792]{1,0:T(8,128)} %copy-done) | copy-start | bytes 2752516
  360.0 3.8 collective-permute-start.1
  367.5 7.2 %collective-permute-start.1 = (bf16[128,1792]{1,0:T(8,128)(2,1)S(1)}, bf16[128,1792]{1,0:T(8,128)(2,1)}, u32[]{:S(2)}, u32[]{:S(2)}) collective-permute-start(bf16[128,1792]{1,0:T(8,128)(2,1)S(1)} %get-tuple-element.465), channel_id=1, source_target_pairs={{32,0},{64,32},{96,64},{128,96},{160,128},{192,160},{224,192},{33,... | collective-permute-start | bytes 1376264 | tf_op jit(solution)/shard_map/while/body/eval_jaxpr/ppermute | solution.py:12
  378.5 9.9 %collective-permute-start.1 = (bf16[128,1792]{1,0:T(8,128)(2,1)S(1)}, bf16[128,1792]{1,0:T(8,128)(2,1)}, u32[]{:S(2)}, u32[]{:S(2)}) collective-permute-start(bf16[128,1792]{1,0:T(8,128)(2,1)S(1)} %get-tuple-element.465), channel_id=1, source_target_pairs={{32,0},{64,32},{96,64},{128,96},{160,128},{192,160},{224,192},{33,... | collective-permute-start | bytes 1376264 | tf_op jit(solution)/shard_map/while/body/eval_jaxpr/ppermute | solution.py:12
  392.1 9.9 %collective-permute-start.1 = (bf16[128,1792]{1,0:T(8,128)(2,1)S(1)}, bf16[128,1792]{1,0:T(8,128)(2,1)}, u32[]{:S(2)}, u32[]{:S(2)}) collective-permute-start(bf16[128,1792]{1,0:T(8,128)(2,1)S(1)} %get-tuple-element.465), channel_id=1, source_target_pairs={{32,0},{64,32},{96,64},{128,96},{160,128},{192,160},{224,192},{33,... | collective-permute-start | bytes 1376264 | tf_op jit(solution)/shard_map/while/body/eval_jaxpr/ppermute | solution.py:12
  405.7 9.9 %collective-permute-start.1 = (bf16[128,1792]{1,0:T(8,128)(2,1)S(1)}, bf16[128,1792]{1,0:T(8,128)(2,1)}, u32[]{:S(2)}, u32[]{:S(2)}) collective-permute-start(bf16[128,1792]{1,0:T(8,128)(2,1)S(1)} %get-tuple-element.465), channel_id=1, source_target_pairs={{32,0},{64,32},{96,64},{128,96},{160,128},{192,160},{224,192},{33,... | collective-permute-start | bytes 1376264 | tf_op jit(solution)/shard_map/while/body/eval_jaxpr/ppermute | solution.py:12
  419.3 9.9 %collective-permute-start.1 = (bf16[128,1792]{1,0:T(8,128)(2,1)S(1)}, bf16[128,1792]{1,0:T(8,128)(2,1)}, u32[]{:S(2)}, u32[]{:S(2)}) collective-permute-start(bf16[128,1792]{1,0:T(8,128)(2,1)S(1)} %get-tuple-element.465), channel_id=1, source_target_pairs={{32,0},{64,32},{96,64},{128,96},{160,128},{192,160},{224,192},{33,... | collective-permute-start | bytes 1376264 | tf_op jit(solution)/shard_map/while/body/eval_jaxpr/ppermute | solution.py:12
  433.0 9.9 %collective-permute-start.1 = (bf16[128,1792]{1,0:T(8,128)(2,1)S(1)}, bf16[128,1792]{1,0:T(8,128)(2,1)}, u32[]{:S(2)}, u32[]{:S(2)}) collective-permute-start(bf16[128,1792]{1,0:T(8,128)(2,1)S(1)} %get-tuple-element.465), channel_id=1, source_target_pairs={{32,0},{64,32},{96,64},{128,96},{160,128},{192,160},{224,192},{33,... | collective-permute-start | bytes 1376264 | tf_op jit(solution)/shard_map/while/body/eval_jaxpr/ppermute | solution.py:12
  446.6 9.9 %collective-permute-start.1 = (bf16[128,1792]{1,0:T(8,128)(2,1)S(1)}, bf16[128,1792]{1,0:T(8,128)(2,1)}, u32[]{:S(2)}, u32[]{:S(2)}) collective-permute-start(bf16[128,1792]{1,0:T(8,128)(2,1)S(1)} %get-tuple-element.465), channel_id=1, source_target_pairs={{32,0},{64,32},{96,64},{128,96},{160,128},{192,160},{224,192},{33,... | collective-permute-start | bytes 1376264 | tf_op jit(solution)/shard_map/while/body/eval_jaxpr/ppermute | solution.py:12
Sparse Core Ops, SparseCore 0:
  11.7 136.3 all-gather.1
  276.8 74.2 all-reduce.1
where the time goes:
time: 677 us; the launch traced here: 676 us
  waiting for transfers between devices  293 us (43%)
  blocking collectives  211 us (31%)
  starting transfers between devices  100 us (15%)
  other arithmetic  41 us (6%)
  matrix products  15.7 us (2%)
  between operations  14.1 us (2%)
    psum x1, blocking collectives, on_device(): grad_threshold = lax.psum(grad_local, ('tm', 'tok'))  211 us
    all_gather x1, waiting for transfers between devices, on_device(): piece = lax.all_gather(gate_weight, ('tm', 'tok'), axis=0, tiled=True)  140 us
    ppermute x16, starting transfers between devices, passed_along(): return lax.ppermute(x, axis, pairs)  100 us
    ppermute x16, waiting for transfers between devices, passed_along(): return lax.ppermute(x, axis, pairs)  77.7 us
    psum x1, waiting for transfers between devices, on_device(): total = lax.psum(spikes, 'tm')  74.4 us
    convert_element_type x8, other arithmetic, backward_turn(): passed_along((incoming + dwide).astype(jnp.bfloat16), 'tm', -1)  16.3 us
  transfers between devices with their start and end apart: 18, of which 18 were waited for; matrix products, arithmetic and copies ran while one was open for 0% of the time, Pallas kernels for 0%

commit v1 on v0

--- a/solution.py
+++ b/solution.py
@@ -19,7 +19,12 @@
     rows = features.shape[0]
     width = gate_weight.shape[1]
     driven = jnp.where(spike_mask[0] > 0, features, jnp.zeros_like(features))
-    piece = lax.all_gather(gate_weight, ("tm", "tok"), axis=0, tiled=True)
+    piece = jnp.concatenate(
+        lax.all_to_all(
+            jnp.stack([gate_weight] * lax.axis_size(("tm", "tok"))), ("tm", "tok"), 0, 0
+        ),
+        axis=0,
+    )
     student = jnp.dot(driven, piece, preferred_element_type=jnp.float32)
     teacher = jnp.dot(features, piece, preferred_element_type=jnp.float32)
     current = 2.0 * student

time: 677 us -> 882 us (1.30)
  waiting for transfers between devices: 293 us -> 484 us
    all_to_all x0 -> x1, waiting for transfers between devices: none -> 288 us  [on_device(): lax.all_to_all(jnp.stack([gate_weight] * lax.axis_size(('tm', 'tok'))), (...]
    all_gather x1 -> x0, waiting for transfers between devices: 140 us -> none  [on_device(): piece = lax.all_gather(gate_weight, ('tm', 'tok'), axis=0, tiled=True)]
    psum x1, waiting for transfers between devices: 74.4 us -> 118 us  [on_device(): total = lax.psum(spikes, 'tm')]
    all_to_all x0 -> x1, starting transfers between devices: none -> 14 us  [on_device(): lax.all_to_all(jnp.stack([gate_weight] * lax.axis_size(('tm', 'tok'))), (...]
where the time goes in v1:
time: 882 us; the launch traced here: 881 us
  waiting for transfers between devices  484 us (55%)
  blocking collectives  211 us (24%)
  starting transfers between devices  108 us (12%)
  other arithmetic  41 us (5%)
  matrix products  15.5 us (2%)
  between operations  14.1 us (2%)
    all_to_all x1, waiting for transfers between devices, on_device(): lax.all_to_all(jnp.stack([gate_weight] * lax.axis_size(('tm', 'tok'))), (...  288 us
    psum x1, blocking collectives, on_device(): grad_threshold = lax.psum(grad_local, ('tm', 'tok'))  211 us
    psum x1, waiting for transfers between devices, on_device(): total = lax.psum(spikes, 'tm')  118 us
    ppermute x16, starting transfers between devices, passed_along(): return lax.ppermute(x, axis, pairs)  93.5 us
    ppermute x16, waiting for transfers between devices, passed_along(): return lax.ppermute(x, axis, pairs)  77.7 us
  transfers between devices with their start and end apart: 18, of which 18 were waited for; matrix products, arithmetic and copies ran while one was open for 0% of the time, Pallas kernels for 0%

profile of v1, /device:TPU:32, one launch (start us, length us, event | category | flops | bytes accessed | tf_op | source)
XLA Modules:
  0.0 880.5 jit_solution(4498688554805008026)
XLA Ops:
  7.2 6.4 stack.2
  13.5 14.0 %all-to-all-start = ((bf16[64,56,1792]{2,1,0:T(8,128)(2,1)}), bf16[64,56,1792]{2,1,0:T(8,128)(2,1)}, u32[]{:S(2)}, u32[]{:S(2)}) async-start(bf16[64,56,1792]{2,1,0:T(8,128)(2,1)} %stack.2), calls=%async_computation | async-start | bytes 25690112 | tf_op jit(solution)/shard_map/all_to_all | solution.py:23
  27.6 288.4 %all-to-all-done = bf16[64,56,1792]{2,1,0:T(8,128)(2,1)} async-done(((bf16[64,56,1792]{2,1,0:T(8,128)(2,1)}), bf16[64,56,1792]{2,1,0:T(8,128)(2,1)}, u32[]{:S(2)}, u32[]{:S(2)}) %all-to-all-start) | async-done | bytes 12845088 | tf_op jit(solution)/shard_map/all_to_all | solution.py:23
  316.1 7.1 convolution_multiply_fusion
  323.3 113.5 %while.34 = (s32[]{:T(128)}, f32[128,1792]{1,0:T(8,128)S(1)}, f32[128,1792]{1,0:T(8,128)S(1)}, f32[128,1792]{1,0:T(8,128)S(1)}, f32[1792]{0:T(1024)S(1)}, /*index=5*/s32[]{:T(128)}, s32[]{:T(128)}, s32[]{:T(128)}) while((s32[]{:T(128)}, f32[128,1792]{1,0:T(8,128)S(1)}, f32[128,1792]{1,0:T(8,128)S(1)}, f32[128,1792]{1,0:T(8,128)S(1)}, ...), condition=%wide.region_1.2_spmd.clone, body=%wide.region_0.1_spmd.clone.sunk | while | flops 2293767 | bytes 8264873 | solution.py:49
  323.3 1.5 select_select_fusion.2
  326.2 2.2 collective-permute-done
  330.0 5.8 collective-permute-start
  335.8 2.2 collective-permute-done
  339.6 12.7 %collective-permute-start = (f32[128,1792]{1,0:T(8,128)}, f32[128,1792]{1,0:T(8,128)S(1)}, u32[]{:S(2)}, u32[]{:S(2)}) collective-permute-start(f32[128,1792]{1,0:T(8,128)} %get-tuple-element.455), channel_id=1, source_target_pairs={{0,32},{32,64},{64,96},{96,128},{128,160},{160,192},{192,224},{1,3... | collective-permute-start | bytes 2752520 | tf_op jit(solution)/shard_map/while/body/eval_jaxpr/ppermute | solution.py:12
  352.3 2.2 collective-permute-done
  356.0 12.7 %collective-permute-start = (f32[128,1792]{1,0:T(8,128)}, f32[128,1792]{1,0:T(8,128)S(1)}, u32[]{:S(2)}, u32[]{:S(2)}) collective-permute-start(f32[128,1792]{1,0:T(8,128)} %get-tuple-element.455), channel_id=1, source_target_pairs={{0,32},{32,64},{64,96},{96,128},{128,160},{160,192},{192,224},{1,3... | collective-permute-start | bytes 2752520 | tf_op jit(solution)/shard_map/while/body/eval_jaxpr/ppermute | solution.py:12
  368.7 2.2 collective-permute-done
  372.5 12.7 %collective-permute-start = (f32[128,1792]{1,0:T(8,128)}, f32[128,1792]{1,0:T(8,128)S(1)}, u32[]{:S(2)}, u32[]{:S(2)}) collective-permute-start(f32[128,1792]{1,0:T(8,128)} %get-tuple-element.455), channel_id=1, source_target_pairs={{0,32},{32,64},{64,96},{96,128},{128,160},{160,192},{192,224},{1,3... | collective-permute-start | bytes 2752520 | tf_op jit(solution)/shard_map/while/body/eval_jaxpr/ppermute | solution.py:12
  385.2 2.2 collective-permute-done
  389.0 12.7 %collective-permute-start = (f32[128,1792]{1,0:T(8,128)}, f32[128,1792]{1,0:T(8,128)S(1)}, u32[]{:S(2)}, u32[]{:S(2)}) collective-permute-start(f32[128,1792]{1,0:T(8,128)} %get-tuple-element.455), channel_id=1, source_target_pairs={{0,32},{32,64},{64,96},{96,128},{128,160},{160,192},{192,224},{1,3... | collective-permute-start | bytes 2752520 | tf_op jit(solution)/shard_map/while/body/eval_jaxpr/ppermute | solution.py:12
  401.6 2.2 collective-permute-done
  405.4 12.7 %collective-permute-start = (f32[128,1792]{1,0:T(8,128)}, f32[128,1792]{1,0:T(8,128)S(1)}, u32[]{:S(2)}, u32[]{:S(2)}) collective-permute-start(f32[128,1792]{1,0:T(8,128)} %get-tuple-element.455), channel_id=1, source_target_pairs={{0,32},{32,64},{64,96},{96,128},{128,160},{160,192},{192,224},{1,3... | collective-permute-start | bytes 2752520 | tf_op jit(solution)/shard_map/while/body/eval_jaxpr/ppermute | solution.py:12
  418.1 2.2 collective-permute-done
  421.9 12.7 %collective-permute-start = (f32[128,1792]{1,0:T(8,128)}, f32[128,1792]{1,0:T(8,128)S(1)}, u32[]{:S(2)}, u32[]{:S(2)}) collective-permute-start(f32[128,1792]{1,0:T(8,128)} %get-tuple-element.455), channel_id=1, source_target_pairs={{0,32},{32,64},{64,96},{96,128},{128,160},{160,192},{192,224},{1,3... | collective-permute-start | bytes 2752520 | tf_op jit(solution)/shard_map/while/body/eval_jaxpr/ppermute | solution.py:12
  434.6 2.2 collective-permute-done
  437.8 117.6 %all-reduce.2.cloned.1.call-done = f32[128,1792]{1,0:T(8,128)} async-done(((f32[128,1792]{1,0:T(8,128)}), f32[128,1792]{1,0:T(8,128)}) %all-reduce.2.cloned.1.call-update) | async-done | bytes 917520 | tf_op jit(solution)/shard_map/psum | solution.py:52
  555.5 8.4 fusion.4
  563.8 99.1 %while.35 = (s32[]{:T(128)}, f32[128,1792]{1,0:T(8,128)}, f32[1792]{0:T(1024)S(1)}, f32[1792]{0:T(1024)S(1)}, f32[128,1792]{1,0:T(8,128)S(1)}, /*index=5*/f32[12...) while((s32[]{:T(128)}, f32[128,1792]{1,0:T(8,128)}, ...), condition=%wide.region_5.6_spmd.clone, body=%wide.region_3.5_spmd.clone.sunk | while | flops 4132359 | bytes 7376058 | solution.py:67
  565.6 2.5 collective-permute-done.1
  568.2 2.0 convert_element_type.22
  570.2 1.7 add_reduce_fusion.2
  573.2 5.9 collective-permute-done.1
  579.1 2.0 convert_element_type.22
  581.1 1.7 add_reduce_fusion.2
  584.1 8.6 collective-permute-done.1
  592.7 2.0 convert_element_type.22
  594.8 1.7 add_reduce_fusion.2
  597.8 8.6 collective-permute-done.1
  606.4 2.0 convert_element_type.22
  608.4 1.7 add_reduce_fusion.2
  611.4 8.6 collective-permute-done.1
  620.0 2.0 convert_element_type.22
  622.0 1.7 add_reduce_fusion.2
  625.0 8.6 collective-permute-done.1
  633.6 2.0 convert_element_type.22
  635.6 1.7 add_reduce_fusion.2
  638.7 8.6 collective-permute-done.1
  647.2 2.0 convert_element_type.22
  649.3 1.7 add_reduce_fusion.2
  652.3 8.6 collective-permute-done.1
  660.9 2.0 convert_element_type.22
  662.9 210.8 %psum.15 = f32[1792]{0:T(1024)} all-reduce(f32[1792]{0:T(1024)S(1)} %get-tuple-element.289), channel_id=1, replica_groups=mesh['tm'=8,'mp'=4,'tok'=8] {'tm','tok'}, use_global_device_ids=true, to_apply=%region_6.7 | all-reduce | flops 1792 | bytes 14336 | tf_op jit(solution)/shard_map/psum | solution.py:70
  (39 shorter events, 24.2 us)
Async XLA Ops:
  13.5 302.6 %copy-start.2 = (bf16[128,3584]{1,0:T(8,128)(2,1)S(1)}, bf16[128,3584]{1,0:T(8,128)(2,1)}, u32[]{:S(2)}) copy-start(bf16[128,3584]{1,0:T(8,128)(2,1)} %param.8) | copy-start | bytes 2752516
  13.5 302.6 %all-to-all-start = ((bf16[64,56,1792]{2,1,0:T(8,128)(2,1)}), bf16[64,56,1792]{2,1,0:T(8,128)(2,1)}, u32[]{:S(2)}, u32[]{:S(2)}) async-start(bf16[64,56,1792]{2,1,0:T(8,128)(2,1)} %stack.2), calls=%async_computation | async-start | bytes 25690112 | tf_op jit(solution)/shard_map/all_to_all | solution.py:23
  27.6 527.9 %all-reduce.2.cloned.1.call-start = ((), (), s32[]{:S(2)}) async-start(), calls=%async_computation.1 | async-start | bytes 1835008 | tf_op jit(solution)/shard_map/psum | solution.py:52
  316.1 7.2 copy-start.3
  324.9 3.6 collective-permute-start
  330.0 8.1 collective-permute-start
  339.6 14.9 %collective-permute-start = (f32[128,1792]{1,0:T(8,128)}, f32[128,1792]{1,0:T(8,128)S(1)}, u32[]{:S(2)}, u32[]{:S(2)}) collective-permute-start(f32[128,1792]{1,0:T(8,128)} %get-tuple-element.455), channel_id=1, source_target_pairs={{0,32},{32,64},{64,96},{96,128},{128,160},{160,192},{192,224},{1,3... | collective-permute-start | bytes 2752520 | tf_op jit(solution)/shard_map/while/body/eval_jaxpr/ppermute | solution.py:12
  356.0 14.9 %collective-permute-start = (f32[128,1792]{1,0:T(8,128)}, f32[128,1792]{1,0:T(8,128)S(1)}, u32[]{:S(2)}, u32[]{:S(2)}) collective-permute-start(f32[128,1792]{1,0:T(8,128)} %get-tuple-element.455), channel_id=1, source_target_pairs={{0,32},{32,64},{64,96},{96,128},{128,160},{160,192},{192,224},{1,3... | collective-permute-start | bytes 2752520 | tf_op jit(solution)/shard_map/while/body/eval_jaxpr/ppermute | solution.py:12
  372.5 14.9 %collective-permute-start = (f32[128,1792]{1,0:T(8,128)}, f32[128,1792]{1,0:T(8,128)S(1)}, u32[]{:S(2)}, u32[]{:S(2)}) collective-permute-start(f32[128,1792]{1,0:T(8,128)} %get-tuple-element.455), channel_id=1, source_target_pairs={{0,32},{32,64},{64,96},{96,128},{128,160},{160,192},{192,224},{1,3... | collective-permute-start | bytes 2752520 | tf_op jit(solution)/shard_map/while/body/eval_jaxpr/ppermute | solution.py:12
  389.0 14.9 %collective-permute-start = (f32[128,1792]{1,0:T(8,128)}, f32[128,1792]{1,0:T(8,128)S(1)}, u32[]{:S(2)}, u32[]{:S(2)}) collective-permute-start(f32[128,1792]{1,0:T(8,128)} %get-tuple-element.455), channel_id=1, source_target_pairs={{0,32},{32,64},{64,96},{96,128},{128,160},{160,192},{192,224},{1,3... | collective-permute-start | bytes 2752520 | tf_op jit(solution)/shard_map/while/body/eval_jaxpr/ppermute | solution.py:12
  405.4 14.9 %collective-permute-start = (f32[128,1792]{1,0:T(8,128)}, f32[128,1792]{1,0:T(8,128)S(1)}, u32[]{:S(2)}, u32[]{:S(2)}) collective-permute-start(f32[128,1792]{1,0:T(8,128)} %get-tuple-element.455), channel_id=1, source_target_pairs={{0,32},{32,64},{64,96},{96,128},{128,160},{160,192},{192,224},{1,3... | collective-permute-start | bytes 2752520 | tf_op jit(solution)/shard_map/while/body/eval_jaxpr/ppermute | solution.py:12
  421.9 14.9 %collective-permute-start = (f32[128,1792]{1,0:T(8,128)}, f32[128,1792]{1,0:T(8,128)S(1)}, u32[]{:S(2)}, u32[]{:S(2)}) collective-permute-start(f32[128,1792]{1,0:T(8,128)} %get-tuple-element.455), channel_id=1, source_target_pairs={{0,32},{32,64},{64,96},{96,128},{128,160},{160,192},{192,224},{1,3... | collective-permute-start | bytes 2752520 | tf_op jit(solution)/shard_map/while/body/eval_jaxpr/ppermute | solution.py:12
  436.8 1.0 copy-start
  437.8 126.0 %copy-start.1 = (f32[128,1792]{1,0:T(8,128)S(1)}, f32[128,1792]{1,0:T(8,128)}, u32[]{:S(2)}) copy-start(f32[128,1792]{1,0:T(8,128)} %copy-done) | copy-start | bytes 2752516
  564.3 3.8 collective-permute-start.1
  571.9 7.2 collective-permute-start.1
  582.8 9.9 %collective-permute-start.1 = (bf16[128,1792]{1,0:T(8,128)(2,1)S(1)}, bf16[128,1792]{1,0:T(8,128)(2,1)}, u32[]{:S(2)}, u32[]{:S(2)}) collective-permute-start(bf16[128,1792]{1,0:T(8,128)(2,1)S(1)} %get-tuple-element.465), channel_id=1, source_target_pairs={{32,0},{64,32},{96,64},{128,96},{160,128},{192,160},{224,192},{33,... | collective-permute-start | bytes 1376264 | tf_op jit(solution)/shard_map/while/body/eval_jaxpr/ppermute | solution.py:12
  596.5 9.9 %collective-permute-start.1 = (bf16[128,1792]{1,0:T(8,128)(2,1)S(1)}, bf16[128,1792]{1,0:T(8,128)(2,1)}, u32[]{:S(2)}, u32[]{:S(2)}) collective-permute-start(bf16[128,1792]{1,0:T(8,128)(2,1)S(1)} %get-tuple-element.465), channel_id=1, source_target_pairs={{32,0},{64,32},{96,64},{128,96},{160,128},{192,160},{224,192},{33,... | collective-permute-start | bytes 1376264 | tf_op jit(solution)/shard_map/while/body/eval_jaxpr/ppermute | solution.py:12
  610.1 9.9 %collective-permute-start.1 = (bf16[128,1792]{1,0:T(8,128)(2,1)S(1)}, bf16[128,1792]{1,0:T(8,128)(2,1)}, u32[]{:S(2)}, u32[]{:S(2)}) collective-permute-start(bf16[128,1792]{1,0:T(8,128)(2,1)S(1)} %get-tuple-element.465), channel_id=1, source_target_pairs={{32,0},{64,32},{96,64},{128,96},{160,128},{192,160},{224,192},{33,... | collective-permute-start | bytes 1376264 | tf_op jit(solution)/shard_map/while/body/eval_jaxpr/ppermute | solution.py:12
  623.7 9.9 %collective-permute-start.1 = (bf16[128,1792]{1,0:T(8,128)(2,1)S(1)}, bf16[128,1792]{1,0:T(8,128)(2,1)}, u32[]{:S(2)}, u32[]{:S(2)}) collective-permute-start(bf16[128,1792]{1,0:T(8,128)(2,1)S(1)} %get-tuple-element.465), channel_id=1, source_target_pairs={{32,0},{64,32},{96,64},{128,96},{160,128},{192,160},{224,192},{33,... | collective-permute-start | bytes 1376264 | tf_op jit(solution)/shard_map/while/body/eval_jaxpr/ppermute | solution.py:12
  637.3 9.9 %collective-permute-start.1 = (bf16[128,1792]{1,0:T(8,128)(2,1)S(1)}, bf16[128,1792]{1,0:T(8,128)(2,1)}, u32[]{:S(2)}, u32[]{:S(2)}) collective-permute-start(bf16[128,1792]{1,0:T(8,128)(2,1)S(1)} %get-tuple-element.465), channel_id=1, source_target_pairs={{32,0},{64,32},{96,64},{128,96},{160,128},{192,160},{224,192},{33,... | collective-permute-start | bytes 1376264 | tf_op jit(solution)/shard_map/while/body/eval_jaxpr/ppermute | solution.py:12
  651.0 9.9 %collective-permute-start.1 = (bf16[128,1792]{1,0:T(8,128)(2,1)S(1)}, bf16[128,1792]{1,0:T(8,128)(2,1)}, u32[]{:S(2)}, u32[]{:S(2)}) collective-permute-start(bf16[128,1792]{1,0:T(8,128)(2,1)S(1)} %get-tuple-element.465), channel_id=1, source_target_pairs={{32,0},{64,32},{96,64},{128,96},{160,128},{192,160},{224,192},{33,... | collective-permute-start | bytes 1376264 | tf_op jit(solution)/shard_map/while/body/eval_jaxpr/ppermute | solution.py:12
Sparse Core Ops, SparseCore 0:
  437.9 117.4 all-reduce.1
